TPU v7x, 512 devices: a whole 4x4x16 slice. The times are simulated.
512 devices in a mesh: dp: 32 (over y, x, core), tm: 16 (over z).
Axes of the slice: x: 4, y: 4, z: 16, core: 2. Of those that a mesh axis runs over, the one named last changes fastest.
Arguments:
- phonemes: bfloat16 [32, 256, 1024], P('dp', 'tm'), may hold values from -6 to 6
- durations: int32 [32, 256], P('dp', 'tm'), may hold values from 1 to 32, 2048 in all within a row
- conv_weight: bfloat16 [9, 1024, 2048], P(None, None, 'tm'), may hold values from -0.0625 to 0.0625
- out_weight: bfloat16 [2048, 1024], P('tm', 'dp'), may hold values from -0.125 to 0.125
- norm_gain: float32 [1024], replicated, may hold values from 0.1 to 1.9
Outputs:
- decoded: bfloat16 [32, 2048, 1024], P('dp', 'tm')
Inputs may be any that keep to these rules, and one draw needn't show every extreme that they name: Each utterance's durations sum to 2048, and in each utterance some phoneme lasts exactly 32 frames.
All inputs are finite; a program needn't handle non-finite values. No bound on the sum of `durations` on one device may be relied on, other than what follows from the above.
Results may differ from a plain program's by a relative error of at most 0.015.
Values may be sent and summed in bfloat16 or wider, within the bound.
A program may use at most 64 MiB of HBM per device.

v0:
```python
import jax
import jax.numpy as jnp
from jax import lax
from jax.sharding import PartitionSpec as P

KER = 9
FR = 128


def on_device(phonemes, durations, conv_weight, out_weight, norm_gain):
    margin = KER // 2
    rows_all, lengths_all = (
        lax.all_gather(phonemes, "tm", axis=1, tiled=True),
        lax.all_gather(durations, "tm", axis=1, tiled=True),
    )
    rows_all = rows_all[0]
    phone_lengths = lengths_all[0]
    phone_ends = jnp.cumsum(phone_lengths).astype(jnp.int32)
    phone_starts = phone_ends - phone_lengths
    total_frames = FR * lax.axis_size("tm")
    first_own = lax.axis_index("tm") * FR
    positions = first_own + jnp.arange(FR, dtype=jnp.int32)
    inside = (positions[:, None] >= phone_starts[None, :]) & (
        positions[:, None] < phone_ends[None, :]
    )
    own_rows = jnp.dot(
        inside.astype(jnp.bfloat16), rows_all, preferred_element_type=jnp.float32
    ).astype(jnp.bfloat16)
    frames = lax.all_gather(own_rows, "tm", axis=0, tiled=True)
    padded = jnp.pad(frames, ((margin, margin), (0, 0)))
    pre_act = jnp.zeros((total_frames, conv_weight.shape[2]), jnp.float32)
    for offset in range(KER):
        pre_act = pre_act + jnp.dot(
            padded[offset : offset + total_frames],
            conv_weight[offset],
            preferred_element_type=jnp.float32,
        )
    hidden = jnp.maximum(pre_act, 0.0).astype(jnp.bfloat16)
    columns = lax.all_gather(out_weight, "dp", axis=1, tiled=True)
    reduced = lax.psum_scatter(
        jnp.dot(hidden, columns, preferred_element_type=jnp.float32).astype(jnp.bfloat16),
        "tm",
        scatter_dimension=0,
        tiled=True,
    ).astype(jnp.float32)
    summed = own_rows.astype(jnp.float32) + reduced
    average = jnp.mean(summed, axis=-1, keepdims=True)
    centered = summed - average
    spread = jnp.mean(centered * centered, axis=-1, keepdims=True)
    decoded = centered * lax.rsqrt(spread + 1e-05) * norm_gain
    return decoded.astype(jnp.bfloat16)[None]


def solution(mesh):
    placed = (P("dp", "tm", None), P("dp", "tm"), P(None, None, "tm"), P("tm", "dp"), P())
    return jax.shard_map(
        on_device, mesh=mesh, in_specs=placed, out_specs=P("dp", "tm", None), check_vma=False
    )
```

profile of v0, /device:TPU:8, one launch (start us, length us, event | category | flops | bytes accessed | tf_op | source)
XLA Modules:
  0.0 251.9 jit_solution(1046039252529930426)
XLA Ops:
  6.5 1.3 dynamic-slice
  8.5 0.8 bitcast_dynamic-update-slice_fusion
  9.2 26.7 %all-reduce.1 = s32[256]{0:T(256)S(1)} all-reduce(s32[256]{0:T(256)S(1)} %bitcast_dynamic-update-slice_fusion), channel_id=1, replica_groups=mesh['dp'=32,'tm'=16] {'tm'}, use_global_device_ids=true, to_apply=%add.1 | all-reduce | flops 256 | bytes 2048
  35.9 0.3 reduce-window.9
  36.2 0.1 slice.59
  36.3 0.1 slice_reduce_fusion
  36.5 0.1 fusion.91
  36.6 30.0 %all_gather.13 = bf16[1,256,1024]{2,1,0:T(8,128)(2,1)S(1)} all-gather(bf16[1,16,1024]{2,1,0:T(8,128)(2,1)} %param.5), channel_id=1, replica_groups=mesh['dp'=32,'tm'=16] {'tm'}, dimensions={1}, use_global_device_ids=true | all-gather | bytes 557056 | tf_op jit(solution)/shard_map/all_gather | solution.py:13
  66.6 1.0 convolution_convert_fusion.1
  67.6 24.7 %all_gather.15 = bf16[128,1024]{0,1:T(8,128)(2,1)S(1)} all-gather(bf16[128,32]{0,1:T(8,128)(2,1)} %param.8), channel_id=1, replica_groups=mesh['dp'=32,'tm'=16] {'dp'}, dimensions={1}, use_global_device_ids=true | all-gather | bytes 270336 | tf_op jit(solution)/shard_map/all_gather | solution.py:39
  92.4 51.5 %all-gather.2.cloned.1.call-done = bf16[2048,1024]{1,0:T(8,128)(2,1)} async-done(((bf16[128,1024]{1,0:T(8,128)(2,1)}), bf16[2048,1024]{1,0:T(8,128)(2,1)}) %all-gather.2.cloned.1.call-update) | async-done | bytes 4194320 | tf_op jit(solution)/shard_map/all_gather | solution.py:29
  143.8 3.6 %fusion.12 = f32[2048,128]{1,0:T(8,128)S(1)} fusion(bf16[2048,1024]{1,0:T(8,128)(2,1)} %all-gather.2.cloned.1.call-done, bf16[9,1024,128]{2,1,0:T(8,128)(2,1)} %param.7), kind=kOutput, calls=%fused_computation.12 | convolution fusion | flops 536870912 | bytes 5505024 | tf_op jit(solution)/shard_map/dot_general | solution.py:33
  147.5 1.3 fusion.10
  148.8 1.3 fusion.6
  150.1 1.3 fusion.4
  151.3 1.3 fusion.2
  152.6 1.3 fusion.22
  154.0 1.3 fusion.25
  155.2 2.3 fusion.18
  157.6 6.8 %convolution_convert_fusion = bf16[2048,1024]{1,0:T(8,128)(2,1)} fusion(bf16[128,1024]{0,1:T(8,128)(2,1)S(1)} %all_gather.15, f32[2048,128]{1,0:T(8,128)S(1)} %fusion.18, bf16[2048,1024]{1,0:T(8,128)(2,1)} %all-gather.2.cloned.1.call-done, bf16[9,1024,128]{2,1,0:T(8,128)(2,1)} %param.7), kind=kOutput, calls=%fused_computation.16 | convolution fusion | flops 1076625408 | bytes 9961472 | tf_op jit(solution)/shard_map/dot_general | solution.py:41
  164.3 76.6 %reduce-scatter.2.cloned.1.call-done = bf16[128,1024]{1,0:T(8,128)(2,1)} async-done(((bf16[2048,1024]{1,0:T(8,128)(2,1)}), bf16[128,1024]{1,0:T(8,128)(2,1)}) %reduce-scatter.2.cloned.1.call-update) | async-done | bytes 262160 | tf_op jit(solution)/shard_map/reduce_scatter | solution.py:40
  241.0 1.1 fusion.51
  242.1 1.2 multiply_reduce_fusion
  243.2 1.8 fusion.52
  (19 shorter events, 0.2 us)
Async XLA Ops:
  6.5 137.3 %all-gather.2.cloned.1.call-start = ((), (), s32[]{:S(2)}) async-start(), calls=%async_computation.1 | async-start | bytes 4456448 | tf_op jit(solution)/shard_map/all_gather | solution.py:29
  67.6 173.4 %reduce-scatter.2.cloned.1.call-start = ((), (), s32[]{:S(2)}) async-start(), calls=%async_computation.2 | async-start | bytes 4456448 | tf_op jit(solution)/shard_map/reduce_scatter | solution.py:40
  92.4 55.1 %copy-start.2 = (bf16[9,1024,128]{2,1,0:T(8,128)(2,1)S(1)}, bf16[9,1024,128]{2,1,0:T(8,128)(2,1)}, u32[]{:S(2)}) copy-start(bf16[9,1024,128]{2,1,0:T(8,128)(2,1)} %param.7) | copy-start | bytes 7077892
  143.8 3.7 %copy-start = (bf16[2048,1024]{1,0:T(8,128)(2,1)S(1)}, bf16[2048,1024]{1,0:T(8,128)(2,1)}, u32[]{:S(2)}) copy-start(bf16[2048,1024]{1,0:T(8,128)(2,1)} %all-gather.2.cloned.1.call-done) | copy-start | bytes 12582916
  164.3 76.7 %copy-start.1 = (bf16[128,1024]{1,0:T(8,128)(2,1)S(1)}, bf16[128,1024]{1,0:T(8,128)(2,1)}, u32[]{:S(2)}) copy-start(bf16[128,1024]{1,0:T(8,128)(2,1)} %convolution_convert_fusion.1) | copy-start | bytes 786436
  164.3 78.9 %copy-start.3 = (f32[1024]{0:T(1024)S(1)}, f32[1024]{0:T(1024)}, u32[]{:S(2)}) copy-start(f32[1024]{0:T(1024)} %param.9) | copy-start | bytes 12292
Sparse Core Ops, SparseCore 0:
  67.7 76.0 all-gather.1
  164.5 76.4 reduce-scatter.1
where the time goes:
time: 252 us
  waiting for transfers between devices  128 us (51%)
  blocking collectives  81.4 us (32%)
  matrix products  21.4 us (8%)
  between operations  14.1 us (6%)
  other arithmetic  4.56 us (2%)
    reduce_scatter x1, waiting for transfers between devices, on_device(): lax.psum_scatter(jnp.dot(hidden, columns, preferred_element_type=jnp.floa...  76.6 us
    all_gather x1, waiting for transfers between devices, on_device(): frames = lax.all_gather(own_rows, 'tm', axis=0, tiled=True)  51.5 us
    all_gather x1, blocking collectives, on_device(): lax.all_gather(phonemes, 'tm', axis=1, tiled=True)  30 us
    unnamed x1, blocking collectives  26.7 us
    all_gather x1, blocking collectives, on_device(): columns = lax.all_gather(out_weight, 'dp', axis=1, tiled=True)  24.7 us
    dot_general x8, matrix products, on_device(): jnp.dot(padded[offset:offset + total_frames], conv_weight[offset], prefer...  13.7 us
    dot_general x1, matrix products, on_device(): jnp.dot(hidden, columns, preferred_element_type=jnp.float32)  6.75 us
  transfers between devices with their start and end apart: 2, of which 2 were waited for; matrix products, arithmetic and copies ran while one was open for 0% of the time, Pallas kernels for 0%

commit v1 on v0

v1 whole, which is shorter than its diff:
```python
import jax
import jax.numpy as jnp
from jax import lax
from jax.experimental import pallas as pl
from jax.experimental.pallas import tpu as pltpu
from jax.sharding import PartitionSpec as P

MESH = pl.DeviceIdType.MESH
BF, F32 = jnp.bfloat16, jnp.float32
NZ = 16
NEAR = (0, 1, 15, 2)
TAPS = 9
HALO = TAPS // 2
ROWS = 144


def chunk_of(offset):
    for j in range(4):
        for r in range(4):
            if (NEAR[j] + 4 * r) % NZ == offset:
                return j, r


def kernel(phon_in, dur_in, conv_w, out_w, gain, out,
           phon, dur_own, dur_all, w, zc, w2, hid_out, hid_in, acc,
           w_sem, ps, pr, ds, dr, ws, wr, xs, xr, cs, cr, hs, hr):
    z = lax.axis_index("tm")
    dp = lax.axis_index("dp")
    y, x, c = dp // 8, lax.rem(dp // 2, 4), lax.rem(dp, 2)

    def zpeer(o):
        return (dp, lax.rem(z + o, NZ))

    def xpeer(d):
        return (y * 8 + lax.rem(x + d, 4) * 2 + c, z)

    def ypeer(d):
        return (lax.rem(y + d, 4) * 8 + x * 2 + c, z)

    sibling = (y * 8 + x * 2 + 1 - c, z)

    def remote(src, dst, ssem, rsem, dev):
        return pltpu.make_async_remote_copy(
            src_ref=src, dst_ref=dst, send_sem=ssem, recv_sem=rsem, device_id=dev, device_id_type=MESH)

    barrier = pltpu.get_barrier_semaphore()
    peers = [zpeer(o) for o in range(1, NZ)] + [xpeer(d) for d in (1, 2, 3)] + [ypeer(d) for d in (1, 2, 3)] + [sibling]
    for dev in peers:
        pl.semaphore_signal(barrier, inc=1, device_id=dev, device_id_type=MESH)

    w_copy = pltpu.make_async_copy(conv_w, w, w_sem)
    w_copy.start()

    phon[0, 0] = phon_in[0]
    dur_own[...] = jnp.zeros_like(dur_own)
    dur_own[:, 0:16] = dur_in[...]
    dur_all[0] = dur_own[...]
    eye = (lax.broadcasted_iota(jnp.int32, (32, 32), 0) == lax.broadcasted_iota(jnp.int32, (32, 32), 1))
    w2_own = lax.dot_general(eye.astype(F32).astype(BF), out_w[...], (((1,), (1,)), ((), ())),
                             preferred_element_type=F32).astype(BF)
    w2[y, x, c, 0, :, 0:128] = w2_own[0:16]
    w2[y, x, c, 1, :, 0:128] = w2_own[16:32]

    def far(r):
        return (remote(phon.at[0, 0], phon.at[0, r], ps.at[r], pr.at[r], zpeer(4 * r)),
                remote(w2.at[y, x, c, :, :, pl.ds(0, 128)], w2.at[y, x, c, :, :, pl.ds(128 * r, 128)],
                       ws.at[r], wr.at[r], zpeer(4 * r)))

    def near(j, r):
        i = 4 * j + r
        return (remote(phon.at[0, r], phon.at[j, r], ps.at[i], pr.at[i], zpeer(NEAR[j])),
                remote(w2.at[y, x, c, :, :, pl.ds(128 * r, 128)], w2.at[y, x, c, :, :, pl.ds(128 * i, 128)],
                       ws.at[i], wr.at[i], zpeer(NEAR[j])))

    def dur_copy(o):
        return remote(dur_own, dur_all.at[o], ds.at[o], dr.at[o], zpeer(o))

    pl.semaphore_wait(barrier, len(peers))

    fars = {r: far(r) for r in (2, 1, 3)}
    nears = {(j, r): near(j, r) for j in (1, 2, 3) for r in range(4)}
    durs = [dur_copy(o) for o in range(1, NZ)]
    for r in (2, 1, 3):
        fars[r][0].start()
    for j in (3, 1, 2):
        nears[j, 0][0].start()
    for d in durs:
        d.start()
    for r in (2, 1, 3):
        fars[r][1].start()
    for j in (3, 1, 2):
        nears[j, 0][1].start()
    for r in (1, 3, 2):
        fars[r][0].wait_recv()
        for j in (3, 1, 2):
            nears[j, r][0].start()
    for r in (1, 3, 2):
        fars[r][1].wait_recv()
        for j in (3, 1, 2):
            nears[j, r][1].start()

    def products(j):
        rows = phon[j].reshape(64, 1024)
        for k in range(0, TAPS, 2):
            taps = [w[t] for t in range(k, min(k + 2, TAPS))]
            cols = jnp.concatenate(taps, axis=1) if len(taps) > 1 else taps[0]
            prod = jnp.dot(rows, cols, preferred_element_type=F32)
            high = prod.astype(BF)
            low = (prod - high.astype(F32)).astype(BF)
            width = 128 * len(taps)
            zc[64 * j:64 * j + 64, 128 * k:128 * k + width] = high
            zc[256 + 64 * j:256 + 64 * j + 64, 128 * k:128 * k + width] = low

    w_copy.wait()
    products(0)

    for d in durs:
        d.wait_recv()
    lengths = jnp.concatenate([dur_all[o] for o in range(NZ)], axis=0).astype(F32).astype(BF)
    col = lax.broadcasted_iota(jnp.int32, (1, 256), 1)
    near_slot, far_slot, place = col // 64, lax.rem(col // 16, 4), lax.rem(col, 16)
    near_off = jnp.where(near_slot == 0, 0, jnp.where(near_slot == 1, 1, jnp.where(near_slot == 2, 15, 2)))
    col_off = lax.rem(near_off + 4 * far_slot, NZ)
    col_chunk = lax.rem(z + NZ - col_off, NZ)
    row_chunk = lax.rem(z + NZ - lax.broadcasted_iota(jnp.int32, (NZ, 256), 0), NZ)
    lane = lax.broadcasted_iota(jnp.int32, (128, 256), 0)
    upto = ((lane <= place) & (lane < 16)).astype(F32).astype(BF)
    exact = (lane == place).astype(F32).astype(BF)
    whole = (lane < 16).astype(F32).astype(BF)
    within = jnp.dot(lengths, upto, preferred_element_type=F32)
    single = jnp.dot(lengths, exact, preferred_element_type=F32)
    total = jnp.dot(lengths, whole, preferred_element_type=F32)
    same = row_chunk == col_chunk
    ends = jnp.sum(jnp.where(same, within, jnp.where(row_chunk < col_chunk, total, 0.0)), axis=0, keepdims=True)
    sizes = jnp.sum(jnp.where(same, single, 0.0), axis=0, keepdims=True)
    starts = ends - sizes

    def one_hot(first, count):
        frame = (lax.broadcasted_iota(jnp.int32, (count, 256), 0) + first).astype(F32)
        return jnp.where((frame >= starts) & (frame < ends), 1.0, 0.0).astype(BF)

    for j in (1, 2, 3):
        for r in range(4):
            nears[j, r][0].wait_recv()
        products(j)

    def hidden(o):
        block = lax.rem(z + o, NZ)
        pick = one_hot(block * 128 - HALO, ROWS)
        pick = jnp.concatenate([pick, pick], axis=1)
        total = jnp.zeros((128, 128), F32)
        for k in range(0, TAPS, 2):
            width = 128 * min(2, TAPS - k)
            got = jnp.dot(pick, zc[:, 128 * k:128 * k + width], preferred_element_type=F32)
            total = total + got[k:k + 128, 0:128]
            if width > 128:
                total = total + got[k + 1:k + 129, 128:256]
        return jnp.maximum(total, 0.0).astype(BF)

    def hid_copy(o):
        return remote(hid_out.at[o], hid_in.at[o], hs.at[o], hr.at[o], zpeer(o))

    def send_hidden(i, carry):
        o = lax.rem(8 + 7 * i, NZ)
        hid_out[o] = hidden(o)
        hid_copy(o).start()
        return carry

    lax.fori_loop(0, 4, send_hidden, 0)

    for j in (1, 2, 3):
        for r in range(4):
            nears[j, r][1].wait_recv()
    first = ([remote(w2.at[y, x, c, 0], w2.at[y, x, c, 0], xs.at[d], xr.at[d], xpeer(d)) for d in (1, 2, 3)]
             + [remote(w2.at[y, x, c, 1], w2.at[y, x, c, 1], xs.at[3 + d], xr.at[3 + d], ypeer(d)) for d in (1, 2, 3)])
    for i in (0, 2, 1, 3, 5, 4):
        first[i].start()

    lax.fori_loop(4, 8, send_hidden, 0)

    for d in first:
        d.wait_recv()
    second = ([remote(w2.at[y, :, c, 0], w2.at[y, :, c, 0], xs.at[6 + d], xr.at[6 + d], ypeer(d)) for d in (1, 2, 3)]
              + [remote(w2.at[:, x, c, 1], w2.at[:, x, c, 1], xs.at[9 + d], xr.at[9 + d], xpeer(d)) for d in (1, 2, 3)])
    for i in (0, 2, 1, 3, 5, 4):
        second[i].start()

    def to_sibling(i):
        if i < 4:
            part = w2.at[lax.rem(y + 4 - i, 4), :, c, 0]
        else:
            part = w2.at[:, lax.rem(x + 8 - i, 4), c, 1]
        return remote(part, part, cs.at[i], cr.at[i], sibling)

    cross = [to_sibling(i) for i in range(8)]
    cross[0].start()
    cross[4].start()

    lax.fori_loop(9, NZ, send_hidden, 0)
    hid_in[0] = hidden(0)

    acc[...] = jnp.dot(one_hot(z * 128, 128), phon[...].reshape(256, 1024), preferred_element_type=F32)

    for i in (1, 3, 2):
        second[i - 1].wait_recv()
        cross[i].start()
        second[2 + i].wait_recv()
        cross[4 + i].start()
    for d in cross:
        d.wait_recv()

    order = [(8 + 7 * i) % NZ for i in range(NZ)]
    groups = (order[0:4], order[4:8], [0] + order[9:12], order[12:16])
    for group in groups:
        for o in group:
            if o:
                hid_copy(o).wait_recv()
        left = jnp.concatenate([hid_in[o] for o in group], axis=1)
        slots = [chunk_of(o) for o in group]
        right = jnp.concatenate(
            [w2[:, :, :, :, :, 128 * (4 * j + r):128 * (4 * j + r) + 128].reshape(1024, 128) for j, r in slots], axis=1)
        acc[...] += lax.dot_general(left, right, (((1,), (1,)), ((), ())), preferred_element_type=F32)

    def norm(i, carry):
        rows = pl.ds(pl.multiple_of(i * 16, 16), 16)
        summed = acc[rows, :]
        centered = summed - jnp.mean(summed, axis=-1, keepdims=True)
        spread = jnp.mean(centered * centered, axis=-1, keepdims=True)
        out[0, rows, :] = (centered * lax.rsqrt(spread + 1e-5) * gain[...]).astype(BF)
        return carry

    lax.fori_loop(0, 8, norm, 0)

    for r in (1, 2, 3):
        for d in fars[r]:
            d.wait_send()
    for j in (1, 2, 3):
        for r in range(4):
            for d in nears[j, r]:
                d.wait_send()
    for d in durs + first + second + cross:
        d.wait_send()
    for o in range(1, NZ):
        hid_copy(o).wait_send()


def on_device(phonemes, durations, conv_weight, out_weight, norm_gain):
    vmem = pl.BlockSpec(memory_space=pltpu.VMEM)
    sems = pltpu.SemaphoreType.DMA
    return pl.pallas_call(
        kernel,
        out_shape=jax.ShapeDtypeStruct((1, 128, 1024), BF),
        in_specs=[vmem, vmem, pl.BlockSpec(memory_space=pl.ANY), vmem, vmem],
        out_specs=vmem,
        scratch_shapes=[
            pltpu.VMEM((4, 4, 16, 1024), BF),
            pltpu.VMEM((1, 128), jnp.int32),
            pltpu.VMEM((NZ, 1, 128), jnp.int32),
            pltpu.VMEM((TAPS, 1024, 128), BF),
            pltpu.VMEM((512, TAPS * 128), BF),
            pltpu.VMEM((4, 4, 2, 2, 16, 2048), BF),
            pltpu.VMEM((NZ, 128, 128), BF),
            pltpu.VMEM((NZ, 128, 128), BF),
            pltpu.VMEM((128, 1024), F32),
            sems, sems((16,)), sems((16,)), sems((16,)), sems((16,)), sems((16,)), sems((16,)),
            sems((13,)), sems((13,)), sems((8,)), sems((8,)), sems((16,)), sems((16,)),
        ],
        compiler_params=pltpu.CompilerParams(
            collective_id=0, has_side_effects=True, vmem_limit_bytes=48 * 1024 * 1024),
        cost_estimate=pl.CostEstimate(flops=4_000_000_000, bytes_accessed=4_000_000, transcendentals=0),
    )(phonemes, durations, conv_weight, out_weight, norm_gain.reshape(1, 1024))


def solution(mesh):
    placed = (P("dp", "tm", None), P("dp", "tm"), P(None, None, "tm"), P("tm", "dp"), P())
    return jax.shard_map(
        on_device, mesh=mesh, in_specs=placed, out_specs=P("dp", "tm", None), check_vma=False
    )
```

time: 252 us -> 69.9 us (0.28)
  the two profiles are of different devices: /device:TPU:8 before, /device:TPU:1 now
where the time goes in v1:
time: 69.9 us; the launch traced here: 69.6 us
  Pallas kernels  64.3 us (92%)
  local copies, waits for them, and re-layouts  5.28 us (8%)
    pallas_call x1, Pallas kernels, on_device(): pl.pallas_call(kernel, out_shape=jax.ShapeDtypeStruct((1, 128, 1024), BF)...  64.3 us
    unnamed x10, local copies, waits for them, and re-layouts  5.28 us

profile of v1, /device:TPU:1, one launch (start us, length us, event | category | flops | bytes accessed | tf_op | source)
XLA Modules:
  0.0 69.6 jit_solution(2883186503538263923)
XLA Ops:
  0.0 0.8 %copy.6.out_w = bf16[128,32]{1,0:T(8,128)(2,1)S(1)} copy(bf16[128,32]{0,1:T(8,128)(2,1)} %param.8) | data formatting | bytes 16384 | tf_op args[3]
  0.8 0.0 copy-start
  0.8 1.7 %copy-done = bf16[9,1024,128]{2,1,0:T(8,128)(2,1)S(1)} copy-done((bf16[9,1024,128]{2,1,0:T(8,128)(2,1)S(1)}, bf16[9,1024,128]{2,1,0:T(8,128)(2,1)}, u32[]{:S(2)}) %copy-start) | copy-done | bytes 2359320
  2.5 0.0 copy-start.1
  2.5 0.8 %copy-done.1 = bf16[1,16,1024]{2,1,0:T(8,128)(2,1)S(1)} copy-done((bf16[1,16,1024]{2,1,0:T(8,128)(2,1)S(1)}, bf16[1,16,1024]{2,1,0:T(8,128)(2,1)}, u32[]{:S(2)}) %copy-start.1) | copy-done | bytes 32792
  3.2 0.0 copy-start.2
  3.2 0.7 copy-done.2
  3.9 0.0 copy-start.3
  3.9 0.7 copy-done.3
  4.6 64.3 %shard_map.55 = bf16[1,128,1024]{2,1,0:T(8,128)(2,1)S(1)} custom-call(bf16[1,16,1024]{2,1,0:T(8,128)(2,1)S(1)} %copy-done.1, s32[1,16]{1,0:T(1,128)S(1)} %copy-done.3, bf16[9,1024,128]{2,1,0:T(8,128)(2,1)S(1)} %copy-done, bf16[128,32]{1,0:T(8,128)(2,1)S(1)} %copy.6.out_w, f32[1,1024]{1,0:T(1,128)S(1)} %bitcast.1), custom_call_target="tpu_custom_call" | custom-call | flops 4000000000 | bytes 4000000 | tf_op jit(solution)/shard_map/pallas_call | solution.py:250
  68.9 0.7 %copy.8 = bf16[1,128,1024]{2,1,0:T(8,128)(2,1)} copy(bf16[1,128,1024]{2,1,0:T(8,128)(2,1)S(1)} %shard_map.55) | data formatting | bytes 524288
Async XLA Ops:
  0.8 1.7 %copy-start = (bf16[9,1024,128]{2,1,0:T(8,128)(2,1)S(1)}, bf16[9,1024,128]{2,1,0:T(8,128)(2,1)}, u32[]{:S(2)}) copy-start(bf16[9,1024,128]{2,1,0:T(8,128)(2,1)} %conv_w.1) | copy-start | bytes 7077892
  2.5 0.8 %copy-start.1 = (bf16[1,16,1024]{2,1,0:T(8,128)(2,1)S(1)}, bf16[1,16,1024]{2,1,0:T(8,128)(2,1)}, u32[]{:S(2)}) copy-start(bf16[1,16,1024]{2,1,0:T(8,128)(2,1)} %phon_in.1) | copy-start | bytes 98308
  3.2 0.7 copy-start.2
  3.9 0.7 copy-start.3

commit v2 on v1

--- a/solution.py
+++ b/solution.py
@@ -8,22 +8,17 @@
 MESH = pl.DeviceIdType.MESH
 BF, F32 = jnp.bfloat16, jnp.float32
 NZ = 16
-NEAR = (0, 1, 15, 2)
+ORDER = (0, 1, 15, 2, 14, 5, 11, 3, 13, 4, 12, 6, 10, 7, 9, 8)
+DIRECT = (5, 11, 2, 14, 1, 15)
+ONWARD = {5: ((3, 8), (2, 7), (1, 6), (15, 4)), 11: ((13, 8), (14, 9), (15, 10), (1, 12)), 2: ((1, 3),), 14: ((15, 13),)}
 TAPS = 9
 HALO = TAPS // 2
 ROWS = 144
 
 
-def chunk_of(offset):
-    for j in range(4):
-        for r in range(4):
-            if (NEAR[j] + 4 * r) % NZ == offset:
-                return j, r
-
-
-def kernel(phon_in, dur_in, conv_w, out_w, gain, out,
-           phon, dur_own, dur_all, w, zc, w2, hid_out, hid_in, acc,
-           w_sem, ps, pr, ds, dr, ws, wr, xs, xr, cs, cr, hs, hr):
+def kernel(phon_in, dur_in, conv_w, out_w, gain_in, out,
+           phon, dur_row, dur_own, dur_all, w, w2_own, gain, zc, w2, hid_out, hid_in, acc,
+           in_sem, ps, pr, ds, dr, ws, wr, xs, xr, cs, cr, hs, hr):
     z = lax.axis_index("tm")
     dp = lax.axis_index("dp")
     y, x, c = dp // 8, lax.rem(dp // 2, 4), lax.rem(dp, 2)
@@ -48,59 +43,75 @@
     for dev in peers:
         pl.semaphore_signal(barrier, inc=1, device_id=dev, device_id_type=MESH)
 
-    w_copy = pltpu.make_async_copy(conv_w, w, w_sem)
-    w_copy.start()
-
-    phon[0, 0] = phon_in[0]
+    phon_copy = pltpu.make_async_copy(phon_in.at[0], phon.at[0], in_sem.at[0])
+    dur_load = pltpu.make_async_copy(dur_in, dur_row, in_sem.at[1])
+    w2_copy = pltpu.make_async_copy(out_w, w2_own, in_sem.at[2])
+    gain_copy = pltpu.make_async_copy(gain_in, gain, in_sem.at[3])
+    w_copy = pltpu.make_async_copy(conv_w, w, in_sem.at[4])
+    for d in (phon_copy, dur_load, w2_copy, gain_copy, w_copy):
+        d.start()
+
     dur_own[...] = jnp.zeros_like(dur_own)
-    dur_own[:, 0:16] = dur_in[...]
+    dur_load.wait()
+    dur_own[:, 0:16] = dur_row[...]
     dur_all[0] = dur_own[...]
-    eye = (lax.broadcasted_iota(jnp.int32, (32, 32), 0) == lax.broadcasted_iota(jnp.int32, (32, 32), 1))
-    w2_own = lax.dot_general(eye.astype(F32).astype(BF), out_w[...], (((1,), (1,)), ((), ())),
-                             preferred_element_type=F32).astype(BF)
+    w2_copy.wait()
     w2[y, x, c, 0, :, 0:128] = w2_own[0:16]
     w2[y, x, c, 1, :, 0:128] = w2_own[16:32]
-
-    def far(r):
-        return (remote(phon.at[0, 0], phon.at[0, r], ps.at[r], pr.at[r], zpeer(4 * r)),
-                remote(w2.at[y, x, c, :, :, pl.ds(0, 128)], w2.at[y, x, c, :, :, pl.ds(128 * r, 128)],
-                       ws.at[r], wr.at[r], zpeer(4 * r)))
-
-    def near(j, r):
-        i = 4 * j + r
-        return (remote(phon.at[0, r], phon.at[j, r], ps.at[i], pr.at[i], zpeer(NEAR[j])),
-                remote(w2.at[y, x, c, :, :, pl.ds(128 * r, 128)], w2.at[y, x, c, :, :, pl.ds(128 * i, 128)],
-                       ws.at[i], wr.at[i], zpeer(NEAR[j])))
+    phon_copy.wait()
+
+    def phon_part(o, part):
+        if part is None:
+            return phon.at[ORDER.index(o)]
+        return phon.at[ORDER.index(o), :, pl.ds(512 * part, 512)]
+
+    def w2_part(o, part):
+        lanes = pl.ds(128 * ORDER.index(o), 128)
+        if part is None:
+            return w2.at[y, x, c, :, :, lanes]
+        return w2.at[y, x, c, part, :, lanes]
+
+    def gather(place, ssem, rsem):
+        def copy(held, to, there):
+            part = None if there != 8 else (0 if held == 5 else 1)
+            i = 0 if part == 1 else there
+            return remote(place(held, part), place(there, part), ssem.at[i], rsem.at[i], zpeer(to))
+
+        direct = {o: copy(0, o, o) for o in DIRECT}
+        onward = {held: [copy(held, to, there) for to, there in jobs] for held, jobs in ONWARD.items()}
+        return direct, onward
 
     def dur_copy(o):
         return remote(dur_own, dur_all.at[o], ds.at[o], dr.at[o], zpeer(o))
 
     pl.semaphore_wait(barrier, len(peers))
 
-    fars = {r: far(r) for r in (2, 1, 3)}
-    nears = {(j, r): near(j, r) for j in (1, 2, 3) for r in range(4)}
+    rows_direct, rows_onward = gather(phon_part, ps, pr)
+    cols_direct, cols_onward = gather(w2_part, ws, wr)
     durs = [dur_copy(o) for o in range(1, NZ)]
-    for r in (2, 1, 3):
-        fars[r][0].start()
-    for j in (3, 1, 2):
-        nears[j, 0][0].start()
+    for o in DIRECT:
+        rows_direct[o].start()
     for d in durs:
         d.start()
-    for r in (2, 1, 3):
-        fars[r][1].start()
-    for j in (3, 1, 2):
-        nears[j, 0][1].start()
-    for r in (1, 3, 2):
-        fars[r][0].wait_recv()
-        for j in (3, 1, 2):
-            nears[j, r][0].start()
-    for r in (1, 3, 2):
-        fars[r][1].wait_recv()
-        for j in (3, 1, 2):
-            nears[j, r][1].start()
+    for o in (5, 11):
+        rows_direct[o].wait_recv()
+        for d in rows_onward[o]:
+            d.start()
+    for o in DIRECT:
+        cols_direct[o].start()
+    for o in (2, 14):
+        rows_direct[o].wait_recv()
+        for d in rows_onward[o]:
+            d.start()
+    for o in (5, 11, 2, 14):
+        cols_direct[o].wait_recv()
+        for d in cols_onward[o]:
+            d.start()
+    rows_onward = sum(rows_onward.values(), [])
+    cols_onward = sum(cols_onward.values(), [])
 
     def products(j):
-        rows = phon[j].reshape(64, 1024)
+        rows = phon[4 * j:4 * j + 4].reshape(64, 1024)
         for k in range(0, TAPS, 2):
             taps = [w[t] for t in range(k, min(k + 2, TAPS))]
             cols = jnp.concatenate(taps, axis=1) if len(taps) > 1 else taps[0]
@@ -112,15 +123,18 @@
             zc[256 + 64 * j:256 + 64 * j + 64, 128 * k:128 * k + width] = low
 
     w_copy.wait()
+    for o in (1, 15):
+        rows_direct[o].wait_recv()
     products(0)
 
     for d in durs:
         d.wait_recv()
     lengths = jnp.concatenate([dur_all[o] for o in range(NZ)], axis=0).astype(F32).astype(BF)
     col = lax.broadcasted_iota(jnp.int32, (1, 256), 1)
-    near_slot, far_slot, place = col // 64, lax.rem(col // 16, 4), lax.rem(col, 16)
-    near_off = jnp.where(near_slot == 0, 0, jnp.where(near_slot == 1, 1, jnp.where(near_slot == 2, 15, 2)))
-    col_off = lax.rem(near_off + 4 * far_slot, NZ)
+    slot, place = col // 16, lax.rem(col, 16)
+    col_off = jnp.zeros_like(col)
+    for i, o in enumerate(ORDER):
+        col_off = jnp.where(slot == i, o, col_off)
     col_chunk = lax.rem(z + NZ - col_off, NZ)
     row_chunk = lax.rem(z + NZ - lax.broadcasted_iota(jnp.int32, (NZ, 256), 0), NZ)
     lane = lax.broadcasted_iota(jnp.int32, (128, 256), 0)
@@ -139,9 +153,9 @@
         frame = (lax.broadcasted_iota(jnp.int32, (count, 256), 0) + first).astype(F32)
         return jnp.where((frame >= starts) & (frame < ends), 1.0, 0.0).astype(BF)
 
+    for d in rows_onward:
+        d.wait_recv()
     for j in (1, 2, 3):
-        for r in range(4):
-            nears[j, r][0].wait_recv()
         products(j)
 
     def hidden(o):
@@ -168,9 +182,10 @@
 
     lax.fori_loop(0, 4, send_hidden, 0)
 
-    for j in (1, 2, 3):
-        for r in range(4):
-            nears[j, r][1].wait_recv()
+    for o in (1, 15):
+        cols_direct[o].wait_recv()
+    for d in cols_onward:
+        d.wait_recv()
     first = ([remote(w2.at[y, x, c, 0], w2.at[y, x, c, 0], xs.at[d], xr.at[d], xpeer(d)) for d in (1, 2, 3)]
              + [remote(w2.at[y, x, c, 1], w2.at[y, x, c, 1], xs.at[3 + d], xr.at[3 + d], ypeer(d)) for d in (1, 2, 3)])
     for i in (0, 2, 1, 3, 5, 4):
@@ -216,10 +231,12 @@
             if o:
                 hid_copy(o).wait_recv()
         left = jnp.concatenate([hid_in[o] for o in group], axis=1)
-        slots = [chunk_of(o) for o in group]
+        slots = [ORDER.index(o) for o in group]
         right = jnp.concatenate(
-            [w2[:, :, :, :, :, 128 * (4 * j + r):128 * (4 * j + r) + 128].reshape(1024, 128) for j, r in slots], axis=1)
+            [w2[:, :, :, :, :, 128 * i:128 * i + 128].reshape(1024, 128) for i in slots], axis=1)
         acc[...] += lax.dot_general(left, right, (((1,), (1,)), ((), ())), preferred_element_type=F32)
+
+    gain_copy.wait()
 
     def norm(i, carry):
         rows = pl.ds(pl.multiple_of(i * 16, 16), 16)
@@ -231,13 +248,11 @@
 
     lax.fori_loop(0, 8, norm, 0)
 
-    for r in (1, 2, 3):
-        for d in fars[r]:
-            d.wait_send()
-    for j in (1, 2, 3):
-        for r in range(4):
-            for d in nears[j, r]:
-                d.wait_send()
+    for o in DIRECT:
+        rows_direct[o].wait_send()
+        cols_direct[o].wait_send()
+    for d in rows_onward + cols_onward:
+        d.wait_send()
     for d in durs + first + second + cross:
         d.wait_send()
     for o in range(1, NZ):
@@ -250,25 +265,28 @@
     return pl.pallas_call(
         kernel,
         out_shape=jax.ShapeDtypeStruct((1, 128, 1024), BF),
-        in_specs=[vmem, vmem, pl.BlockSpec(memory_space=pl.ANY), vmem, vmem],
+        in_specs=[pl.BlockSpec(memory_space=pltpu.HBM)] * 5,
         out_specs=vmem,
         scratch_shapes=[
-            pltpu.VMEM((4, 4, 16, 1024), BF),
+            pltpu.VMEM((NZ, 16, 1024), BF),
+            pltpu.VMEM((1, 16), jnp.int32),
             pltpu.VMEM((1, 128), jnp.int32),
             pltpu.VMEM((NZ, 1, 128), jnp.int32),
             pltpu.VMEM((TAPS, 1024, 128), BF),
+            pltpu.VMEM((32, 128), BF),
+            pltpu.VMEM((1, 1024), F32),
             pltpu.VMEM((512, TAPS * 128), BF),
             pltpu.VMEM((4, 4, 2, 2, 16, 2048), BF),
             pltpu.VMEM((NZ, 128, 128), BF),
             pltpu.VMEM((NZ, 128, 128), BF),
             pltpu.VMEM((128, 1024), F32),
-            sems, sems((16,)), sems((16,)), sems((16,)), sems((16,)), sems((16,)), sems((16,)),
+            sems((5,)), sems((16,)), sems((16,)), sems((16,)), sems((16,)), sems((16,)), sems((16,)),
             sems((13,)), sems((13,)), sems((8,)), sems((8,)), sems((16,)), sems((16,)),
         ],
         compiler_params=pltpu.CompilerParams(
-            collective_id=0, has_side_effects=True, vmem_limit_bytes=48 * 1024 * 1024),
+            collective_id=0, has_side_effects=True, vmem_limit_bytes=63 * 1024 * 1024),
         cost_estimate=pl.CostEstimate(flops=4_000_000_000, bytes_accessed=4_000_000, transcendentals=0),
-    )(phonemes, durations, conv_weight, out_weight, norm_gain.reshape(1, 1024))
+    )(phonemes, durations, conv_weight, out_weight.T, norm_gain.reshape(1, 1024))
 
 
 def solution(mesh):

time: 69.9 us -> 67.1 us (0.960)
  local copies, waits for them, and re-layouts: 5.28 us -> 1.67 us
  Pallas kernels: 64.3 us -> 65.3 us
    unnamed x10 -> x1, local copies, waits for them, and re-layouts: 5.28 us -> 1.67 us
    pallas_call x1, Pallas kernels: 64.3 us -> 65.3 us  [on_device(): pl.pallas_call(kernel, out_shape=jax.ShapeDtypeStruct((1, 128, 1024), BF)...]
where the time goes in v2:
time: 67.1 us; the launch traced here: 66.9 us
  Pallas kernels  65.3 us (97%)
  local copies, waits for them, and re-layouts  1.67 us (2%)
    pallas_call x1, Pallas kernels, on_device(): pl.pallas_call(kernel, out_shape=jax.ShapeDtypeStruct((1, 128, 1024), BF)...  65.3 us
    unnamed x1, local copies, waits for them, and re-layouts  1.67 us

profile of v2, /device:TPU:1, one launch (start us, length us, event | category | flops | bytes accessed | tf_op | source)
XLA Modules:
  0.0 66.9 jit_solution(321893294027460099)
XLA Ops:
  0.0 65.3 %shard_map.55 = bf16[1,128,1024]{2,1,0:T(8,128)(2,1)} custom-call(bf16[1,16,1024]{2,1,0:T(8,128)(2,1)} %phon_in.1, s32[1,16]{1,0:T(1,128)} %dur_in.1, bf16[9,1024,128]{2,1,0:T(8,128)(2,1)} %conv_w.1, bf16[32,128]{1,0:T(8,128)(2,1)} %bitcast.2, f32[1,1024]{1,0:T(1,128)} %bitcast.3), custom_call_target="tpu_custom_call" | custom-call | flops 4000000000 | bytes 4000000 | tf_op jit(solution)/shard_map/pallas_call | solution.py:265
  65.3 1.7 %copy.7 = bf16[1,128,1024]{2,1,0:T(8,128)(2,1)} copy(bf16[1,128,1024]{2,1,0:T(8,128)(2,1)} %shard_map.55) | data formatting | bytes 524288

commit v3 on v2

--- a/solution.py
+++ b/solution.py
@@ -90,25 +90,24 @@
     cols_direct, cols_onward = gather(w2_part, ws, wr)
     durs = [dur_copy(o) for o in range(1, NZ)]
     for o in DIRECT:
+        cols_direct[o].start()
+    for o in DIRECT:
         rows_direct[o].start()
     for d in durs:
         d.start()
-    for o in (5, 11):
-        rows_direct[o].wait_recv()
-        for d in rows_onward[o]:
-            d.start()
-    for o in DIRECT:
-        cols_direct[o].start()
-    for o in (2, 14):
-        rows_direct[o].wait_recv()
-        for d in rows_onward[o]:
-            d.start()
     for o in (5, 11, 2, 14):
         cols_direct[o].wait_recv()
         for d in cols_onward[o]:
             d.start()
-    rows_onward = sum(rows_onward.values(), [])
-    cols_onward = sum(cols_onward.values(), [])
+        rows_direct[o].wait_recv()
+        for d in rows_onward[o]:
+            d.start()
+
+    def wait_rows(o):
+        for held, jobs in ONWARD.items():
+            for job, d in zip(jobs, rows_onward[held]):
+                if job[1] == o:
+                    d.wait_recv()
 
     def products(j):
         rows = phon[4 * j:4 * j + 4].reshape(64, 1024)
@@ -123,9 +122,22 @@
             zc[256 + 64 * j:256 + 64 * j + 64, 128 * k:128 * k + width] = low
 
     w_copy.wait()
-    for o in (1, 15):
-        rows_direct[o].wait_recv()
+    rows_direct[1].wait_recv()
+    rows_direct[15].wait_recv()
     products(0)
+
+    cols_direct[1].wait_recv()
+    cols_direct[15].wait_recv()
+    for jobs in cols_onward.values():
+        for d in jobs:
+            d.wait_recv()
+    first = ([remote(w2.at[y, x, c, 0], w2.at[y, x, c, 0], xs.at[d], xr.at[d], xpeer(d)) for d in (1, 2, 3)]
+             + [remote(w2.at[y, x, c, 1], w2.at[y, x, c, 1], xs.at[3 + d], xr.at[3 + d], ypeer(d)) for d in (1, 2, 3)])
+    for i in (0, 2, 1, 3, 5, 4):
+        first[i].start()
+
+    wait_rows(3)
+    products(1)
 
     for d in durs:
         d.wait_recv()
@@ -153,9 +165,9 @@
         frame = (lax.broadcasted_iota(jnp.int32, (count, 256), 0) + first).astype(F32)
         return jnp.where((frame >= starts) & (frame < ends), 1.0, 0.0).astype(BF)
 
-    for d in rows_onward:
-        d.wait_recv()
-    for j in (1, 2, 3):
+    for j in (2, 3):
+        for o in ORDER[4 * j:4 * j + 4]:
+            wait_rows(o)
         products(j)
 
     def hidden(o):
@@ -182,17 +194,6 @@
 
     lax.fori_loop(0, 4, send_hidden, 0)
 
-    for o in (1, 15):
-        cols_direct[o].wait_recv()
-    for d in cols_onward:
-        d.wait_recv()
-    first = ([remote(w2.at[y, x, c, 0], w2.at[y, x, c, 0], xs.at[d], xr.at[d], xpeer(d)) for d in (1, 2, 3)]
-             + [remote(w2.at[y, x, c, 1], w2.at[y, x, c, 1], xs.at[3 + d], xr.at[3 + d], ypeer(d)) for d in (1, 2, 3)])
-    for i in (0, 2, 1, 3, 5, 4):
-        first[i].start()
-
-    lax.fori_loop(4, 8, send_hidden, 0)
-
     for d in first:
         d.wait_recv()
     second = ([remote(w2.at[y, :, c, 0], w2.at[y, :, c, 0], xs.at[6 + d], xr.at[6 + d], ypeer(d)) for d in (1, 2, 3)]
@@ -211,6 +212,7 @@
     cross[0].start()
     cross[4].start()
 
+    lax.fori_loop(4, 8, send_hidden, 0)
     lax.fori_loop(9, NZ, send_hidden, 0)
     hid_in[0] = hidden(0)
 
@@ -251,8 +253,9 @@
     for o in DIRECT:
         rows_direct[o].wait_send()
         cols_direct[o].wait_send()
-    for d in rows_onward + cols_onward:
-        d.wait_send()
+    for jobs in [*rows_onward.values(), *cols_onward.values()]:
+        for d in jobs:
+            d.wait_send()
     for d in durs + first + second + cross:
         d.wait_send()
     for o in range(1, NZ):

time: 67.1 us -> 63.1 us (0.940)
  Pallas kernels: 65.3 us -> 60.6 us
    pallas_call x1, Pallas kernels: 65.3 us -> 60.6 us  [on_device(): pl.pallas_call(kernel, out_shape=jax.ShapeDtypeStruct((1, 128, 1024), BF)...]
where the time goes in v3:
time: 63.1 us; the launch traced here: 62.3 us
  Pallas kernels  60.6 us (96%)
  local copies, waits for them, and re-layouts  1.67 us (3%)
    pallas_call x1, Pallas kernels, on_device(): pl.pallas_call(kernel, out_shape=jax.ShapeDtypeStruct((1, 128, 1024), BF)...  60.6 us
    unnamed x1, local copies, waits for them, and re-layouts  1.67 us

profile of v3, /device:TPU:1, one launch (start us, length us, event | category | flops | bytes accessed | tf_op | source)
XLA Modules:
  0.0 62.3 jit_solution(14894181475456132264)
XLA Ops:
  0.0 60.6 %shard_map.55 = bf16[1,128,1024]{2,1,0:T(8,128)(2,1)} custom-call(bf16[1,16,1024]{2,1,0:T(8,128)(2,1)} %phon_in.1, s32[1,16]{1,0:T(1,128)} %dur_in.1, bf16[9,1024,128]{2,1,0:T(8,128)(2,1)} %conv_w.1, bf16[32,128]{1,0:T(8,128)(2,1)} %bitcast.2, f32[1,1024]{1,0:T(1,128)} %bitcast.3), custom_call_target="tpu_custom_call" | custom-call | flops 4000000000 | bytes 4000000 | tf_op jit(solution)/shard_map/pallas_call | solution.py:268
  60.6 1.7 %copy.7 = bf16[1,128,1024]{2,1,0:T(8,128)(2,1)} copy(bf16[1,128,1024]{2,1,0:T(8,128)(2,1)} %shard_map.55) | data formatting | bytes 524288

commit v4 on v3

--- a/solution.py
+++ b/solution.py
@@ -8,16 +8,19 @@
 MESH = pl.DeviceIdType.MESH
 BF, F32 = jnp.bfloat16, jnp.float32
 NZ = 16
-ORDER = (0, 1, 15, 2, 14, 5, 11, 3, 13, 4, 12, 6, 10, 7, 9, 8)
-DIRECT = (5, 11, 2, 14, 1, 15)
-ONWARD = {5: ((3, 8), (2, 7), (1, 6), (15, 4)), 11: ((13, 8), (14, 9), (15, 10), (1, 12)), 2: ((1, 3),), 14: ((15, 13),)}
+ORDER = (0, 1, 15, 3, 13, 4, 12, 2, 14, 6, 10, 7, 9, 5, 11, 8)
+DIRECT = (3, 13, 1, 15)
+ONWARD = {3: ((3, 6), (1, 4), (15, 2)), 13: ((13, 10), (15, 12), (1, 14)),
+          6: ((2, 8), (1, 7), (15, 5)), 10: ((14, 8), (15, 9), (1, 11))}
+GROUPS = ((0, 5), (5, 11), (11, 16))
+WAVES = ((0, 11), (11, 16))
 TAPS = 9
 HALO = TAPS // 2
 ROWS = 144
 
 
 def kernel(phon_in, dur_in, conv_w, out_w, gain_in, out,
-           phon, dur_row, dur_own, dur_all, w, w2_own, gain, zc, w2, hid_out, hid_in, acc,
+           phon, dur_row, dur_all, w, w2_own, gain, zc, w2, hid_out, hid_in, acc,
            in_sem, ps, pr, ds, dr, ws, wr, xs, xr, cs, cr, hs, hr):
     z = lax.axis_index("tm")
     dp = lax.axis_index("dp")
@@ -39,7 +42,7 @@
             src_ref=src, dst_ref=dst, send_sem=ssem, recv_sem=rsem, device_id=dev, device_id_type=MESH)
 
     barrier = pltpu.get_barrier_semaphore()
-    peers = [zpeer(o) for o in range(1, NZ)] + [xpeer(d) for d in (1, 2, 3)] + [ypeer(d) for d in (1, 2, 3)] + [sibling]
+    peers = [zpeer(o) for o in (1, 2, 3, 13, 14, 15)] + [xpeer(d) for d in (1, 2, 3)] + [ypeer(d) for d in (1, 2, 3)] + [sibling]
     for dev in peers:
         pl.semaphore_signal(barrier, inc=1, device_id=dev, device_id_type=MESH)
 
@@ -51,10 +54,9 @@
     for d in (phon_copy, dur_load, w2_copy, gain_copy, w_copy):
         d.start()
 
-    dur_own[...] = jnp.zeros_like(dur_own)
+    dur_all[0] = jnp.zeros((1, 128), jnp.int32)
     dur_load.wait()
-    dur_own[:, 0:16] = dur_row[...]
-    dur_all[0] = dur_own[...]
+    dur_all[0, :, 0:16] = dur_row[...]
     w2_copy.wait()
     w2[y, x, c, 0, :, 0:128] = w2_own[0:16]
     w2[y, x, c, 1, :, 0:128] = w2_own[16:32]
@@ -71,46 +73,45 @@
             return w2.at[y, x, c, :, :, lanes]
         return w2.at[y, x, c, part, :, lanes]
 
-    def gather(place, ssem, rsem):
+    def dur_part(o, part):
+        return dur_all.at[o]
+
+    def gather(place, ssem, rsem, halves=True):
         def copy(held, to, there):
-            part = None if there != 8 else (0 if held == 5 else 1)
+            part = None if there != 8 or not halves else (0 if held == 6 else 1)
             i = 0 if part == 1 else there
             return remote(place(held, part), place(there, part), ssem.at[i], rsem.at[i], zpeer(to))
 
-        direct = {o: copy(0, o, o) for o in DIRECT}
-        onward = {held: [copy(held, to, there) for to, there in jobs] for held, jobs in ONWARD.items()}
-        return direct, onward
-
-    def dur_copy(o):
-        return remote(dur_own, dur_all.at[o], ds.at[o], dr.at[o], zpeer(o))
+        direct = {o: [copy(0, o, o)] for o in DIRECT}
+        onward = {held: [copy(held, to, there) for to, there in jobs if halves or (held, there) != (10, 8)]
+                  for held, jobs in ONWARD.items()}
+        arrival = dict(direct)
+        for held, jobs in ONWARD.items():
+            for job, d in zip(jobs[::-1], onward[held][::-1]):
+                arrival[job[1]] = arrival.get(job[1], []) + [d]
+        return direct, onward, arrival
 
     pl.semaphore_wait(barrier, len(peers))
 
-    rows_direct, rows_onward = gather(phon_part, ps, pr)
-    cols_direct, cols_onward = gather(w2_part, ws, wr)
-    durs = [dur_copy(o) for o in range(1, NZ)]
-    for o in DIRECT:
-        cols_direct[o].start()
-    for o in DIRECT:
-        rows_direct[o].start()
-    for d in durs:
-        d.start()
-    for o in (5, 11, 2, 14):
-        cols_direct[o].wait_recv()
-        for d in cols_onward[o]:
-            d.start()
-        rows_direct[o].wait_recv()
-        for d in rows_onward[o]:
-            d.start()
-
-    def wait_rows(o):
-        for held, jobs in ONWARD.items():
-            for job, d in zip(jobs, rows_onward[held]):
-                if job[1] == o:
-                    d.wait_recv()
-
-    def products(j):
-        rows = phon[4 * j:4 * j + 4].reshape(64, 1024)
+    gathers = [gather(w2_part, ws, wr), gather(phon_part, ps, pr), gather(dur_part, ds, dr, False)]
+    cols, rows, durs = [g[2] for g in gathers]
+
+    def arrive(chunks, which):
+        for o in which:
+            for d in chunks.pop(o, []):
+                d.wait_recv()
+
+    for direct, _, _ in gathers:
+        for o in DIRECT:
+            direct[o][0].start()
+    for held in ONWARD:
+        for _, onward, arrival in gathers:
+            arrive(arrival, (held,))
+            for d in onward[held]:
+                d.start()
+
+    def products(begin, end):
+        rows = phon[begin:end].reshape(16 * (end - begin), 1024)
         for k in range(0, TAPS, 2):
             taps = [w[t] for t in range(k, min(k + 2, TAPS))]
             cols = jnp.concatenate(taps, axis=1) if len(taps) > 1 else taps[0]
@@ -118,29 +119,54 @@
             high = prod.astype(BF)
             low = (prod - high.astype(F32)).astype(BF)
             width = 128 * len(taps)
-            zc[64 * j:64 * j + 64, 128 * k:128 * k + width] = high
-            zc[256 + 64 * j:256 + 64 * j + 64, 128 * k:128 * k + width] = low
-
+            zc[16 * begin:16 * end, 128 * k:128 * k + width] = high
+            zc[256 + 16 * begin:256 + 16 * end, 128 * k:128 * k + width] = low
+
+    def spread(i):
+        lanes = pl.ds(128 * WAVES[i][0], 128 * (WAVES[i][1] - WAVES[i][0]))
+        first, second, cross = [], [], []
+        own = [w2.at[y, x, c, h, :, lanes] for h in (0, 1)]
+        row, column = w2.at[y, :, c, 0, :, lanes], w2.at[:, x, c, 1, :, lanes]
+        for d in (1, 3, 2):
+            first.append(remote(own[0], own[0], xs.at[i, d], xr.at[i, d], xpeer(d)))
+            first.append(remote(own[1], own[1], xs.at[i, 3 + d], xr.at[i, 3 + d], ypeer(d)))
+            second.append(remote(row, row, xs.at[i, 6 + d], xr.at[i, 6 + d], ypeer(d)))
+            second.append(remote(column, column, xs.at[i, 9 + d], xr.at[i, 9 + d], xpeer(d)))
+        for d in (0, 1, 3, 2):
+            part = w2.at[lax.rem(y + 4 - d, 4), :, c, 0, :, lanes]
+            cross.append(remote(part, part, cs.at[i, d], cr.at[i, d], sibling))
+            part = w2.at[:, lax.rem(x + 4 - d, 4), c, 1, :, lanes]
+            cross.append(remote(part, part, cs.at[i, 4 + d], cr.at[i, 4 + d], sibling))
+        return first, second, cross
+
+    spreads = [spread(i) for i in range(len(WAVES))]
+
+    def spread_first(i):
+        arrive(cols, ORDER[WAVES[i][0]:WAVES[i][1]])
+        for d in spreads[i][0]:
+            d.start()
+
+    def spread_second(i):
+        first, second, cross = spreads[i]
+        for d in first:
+            d.wait_recv()
+        for d in second + cross[0:2]:
+            d.start()
+
+    def spread_cross(i):
+        _, second, cross = spreads[i]
+        for d, onward in zip(second, cross[2:]):
+            d.wait_recv()
+            onward.start()
+
+    spread_first(0)
     w_copy.wait()
-    rows_direct[1].wait_recv()
-    rows_direct[15].wait_recv()
-    products(0)
-
-    cols_direct[1].wait_recv()
-    cols_direct[15].wait_recv()
-    for jobs in cols_onward.values():
-        for d in jobs:
-            d.wait_recv()
-    first = ([remote(w2.at[y, x, c, 0], w2.at[y, x, c, 0], xs.at[d], xr.at[d], xpeer(d)) for d in (1, 2, 3)]
-             + [remote(w2.at[y, x, c, 1], w2.at[y, x, c, 1], xs.at[3 + d], xr.at[3 + d], ypeer(d)) for d in (1, 2, 3)])
-    for i in (0, 2, 1, 3, 5, 4):
-        first[i].start()
-
-    wait_rows(3)
-    products(1)
-
-    for d in durs:
-        d.wait_recv()
+    for begin, end in GROUPS[0:2]:
+        arrive(rows, ORDER[begin:end])
+        products(begin, end)
+    spread_first(1)
+
+    arrive(durs, range(NZ))
     lengths = jnp.concatenate([dur_all[o] for o in range(NZ)], axis=0).astype(F32).astype(BF)
     col = lax.broadcasted_iota(jnp.int32, (1, 256), 1)
     slot, place = col // 16, lax.rem(col, 16)
@@ -165,10 +191,9 @@
         frame = (lax.broadcasted_iota(jnp.int32, (count, 256), 0) + first).astype(F32)
         return jnp.where((frame >= starts) & (frame < ends), 1.0, 0.0).astype(BF)
 
-    for j in (2, 3):
-        for o in ORDER[4 * j:4 * j + 4]:
-            wait_rows(o)
-        products(j)
+    begin, end = GROUPS[2]
+    arrive(rows, ORDER[begin:end])
+    products(begin, end)
 
     def hidden(o):
         block = lax.rem(z + o, NZ)
@@ -192,39 +217,21 @@
         hid_copy(o).start()
         return carry
 
-    lax.fori_loop(0, 4, send_hidden, 0)
-
-    for d in first:
-        d.wait_recv()
-    second = ([remote(w2.at[y, :, c, 0], w2.at[y, :, c, 0], xs.at[6 + d], xr.at[6 + d], ypeer(d)) for d in (1, 2, 3)]
-              + [remote(w2.at[:, x, c, 1], w2.at[:, x, c, 1], xs.at[9 + d], xr.at[9 + d], xpeer(d)) for d in (1, 2, 3)])
-    for i in (0, 2, 1, 3, 5, 4):
-        second[i].start()
-
-    def to_sibling(i):
-        if i < 4:
-            part = w2.at[lax.rem(y + 4 - i, 4), :, c, 0]
-        else:
-            part = w2.at[:, lax.rem(x + 8 - i, 4), c, 1]
-        return remote(part, part, cs.at[i], cr.at[i], sibling)
-
-    cross = [to_sibling(i) for i in range(8)]
-    cross[0].start()
-    cross[4].start()
-
-    lax.fori_loop(4, 8, send_hidden, 0)
+    lax.fori_loop(0, 3, send_hidden, 0)
+    spread_second(0)
+    lax.fori_loop(3, 6, send_hidden, 0)
+    spread_second(1)
+    lax.fori_loop(6, 8, send_hidden, 0)
     lax.fori_loop(9, NZ, send_hidden, 0)
     hid_in[0] = hidden(0)
 
     acc[...] = jnp.dot(one_hot(z * 128, 128), phon[...].reshape(256, 1024), preferred_element_type=F32)
 
-    for i in (1, 3, 2):
-        second[i - 1].wait_recv()
-        cross[i].start()
-        second[2 + i].wait_recv()
-        cross[4 + i].start()
-    for d in cross:
-        d.wait_recv()
+    for i in range(len(WAVES)):
+        spread_cross(i)
+    for _, _, cross in spreads:
+        for d in cross:
+            d.wait_recv()
 
     order = [(8 + 7 * i) % NZ for i in range(NZ)]
     groups = (order[0:4], order[4:8], [0] + order[9:12], order[12:16])
@@ -250,14 +257,13 @@
 
     lax.fori_loop(0, 8, norm, 0)
 
-    for o in DIRECT:
-        rows_direct[o].wait_send()
-        cols_direct[o].wait_send()
-    for jobs in [*rows_onward.values(), *cols_onward.values()]:
-        for d in jobs:
+    for direct, onward, _ in gathers:
+        for jobs in [*direct.values(), *onward.values()]:
+            for d in jobs:
+                d.wait_send()
+    for first, second, cross in spreads:
+        for d in first + second + cross:
             d.wait_send()
-    for d in durs + first + second + cross:
-        d.wait_send()
     for o in range(1, NZ):
         hid_copy(o).wait_send()
 
@@ -267,13 +273,12 @@
     sems = pltpu.SemaphoreType.DMA
     return pl.pallas_call(
         kernel,
-        out_shape=jax.ShapeDtypeStruct((1, 128, 1024), BF),
+        out_shape=pltpu.VMEM((1, 128, 1024), BF),
         in_specs=[pl.BlockSpec(memory_space=pltpu.HBM)] * 5,
         out_specs=vmem,
         scratch_shapes=[
             pltpu.VMEM((NZ, 16, 1024), BF),
             pltpu.VMEM((1, 16), jnp.int32),
-            pltpu.VMEM((1, 128), jnp.int32),
             pltpu.VMEM((NZ, 1, 128), jnp.int32),
             pltpu.VMEM((TAPS, 1024, 128), BF),
             pltpu.VMEM((32, 128), BF),
@@ -284,7 +289,7 @@
             pltpu.VMEM((NZ, 128, 128), BF),
             pltpu.VMEM((128, 1024), F32),
             sems((5,)), sems((16,)), sems((16,)), sems((16,)), sems((16,)), sems((16,)), sems((16,)),
-            sems((13,)), sems((13,)), sems((8,)), sems((8,)), sems((16,)), sems((16,)),
+            sems((2, 13)), sems((2, 13)), sems((2, 8)), sems((2, 8)), sems((16,)), sems((16,)),
         ],
         compiler_params=pltpu.CompilerParams(
             collective_id=0, has_side_effects=True, vmem_limit_bytes=63 * 1024 * 1024),

time: 63.1 us -> 57.8 us (0.916)
  the two profiles are of different devices: /device:TPU:1 before, /device:TPU:6 now
where the time goes in v4:
time: 57.8 us; the launch traced here: 57.6 us
  Pallas kernels  56.9 us (98%)
  local copies, waits for them, and re-layouts  0.71 us (1%)
    pallas_call x1, Pallas kernels, on_device(): pl.pallas_call(kernel, out_shape=pltpu.VMEM((1, 128, 1024), BF), in_specs...  56.9 us

profile of v4, /device:TPU:6, one launch (start us, length us, event | category | flops | bytes accessed | tf_op | source)
XLA Modules:
  0.0 57.6 jit_solution(12383574549017771827)
XLA Ops:
  0.0 56.9 %shard_map.55 = bf16[1,128,1024]{2,1,0:T(8,128)(2,1)S(1)} custom-call(bf16[1,16,1024]{2,1,0:T(8,128)(2,1)} %phon_in.1, s32[1,16]{1,0:T(1,128)} %dur_in.1, bf16[9,1024,128]{2,1,0:T(8,128)(2,1)} %conv_w.1, bf16[32,128]{1,0:T(8,128)(2,1)} %bitcast.2, f32[1,1024]{1,0:T(1,128)} %bitcast.3), custom_call_target="tpu_custom_call" | custom-call | flops 4000000000 | bytes 4000000 | tf_op jit(solution)/shard_map/pallas_call | solution.py:274
  56.9 0.7 %copy.7 = bf16[1,128,1024]{2,1,0:T(8,128)(2,1)} copy(bf16[1,128,1024]{2,1,0:T(8,128)(2,1)S(1)} %shard_map.55) | data formatting | bytes 524288

commit v5 on v4

--- a/solution.py
+++ b/solution.py
@@ -12,6 +12,7 @@
 DIRECT = (3, 13, 1, 15)
 ONWARD = {3: ((3, 6), (1, 4), (15, 2)), 13: ((13, 10), (15, 12), (1, 14)),
           6: ((2, 8), (1, 7), (15, 5)), 10: ((14, 8), (15, 9), (1, 11))}
+GREETED = (1, 2, 3, 13, 14, 15)
 GROUPS = ((0, 5), (5, 11), (11, 16))
 WAVES = ((0, 11), (11, 16))
 TAPS = 9
@@ -20,8 +21,8 @@
 
 
 def kernel(phon_in, dur_in, conv_w, out_w, gain_in, out,
-           phon, dur_row, dur_all, w, w2_own, gain, zc, w2, hid_out, hid_in, acc,
-           in_sem, ps, pr, ds, dr, ws, wr, xs, xr, cs, cr, hs, hr):
+           phon, dur_row, dur_wide, w, w2_own, gain, zc, w2, hid_out, hid_in, acc,
+           in_sem, ps, pr, ws, wr, xs, xr, cs, cr, hs, hr):
     z = lax.axis_index("tm")
     dp = lax.axis_index("dp")
     y, x, c = dp // 8, lax.rem(dp // 2, 4), lax.rem(dp, 2)
@@ -42,11 +43,11 @@
             src_ref=src, dst_ref=dst, send_sem=ssem, recv_sem=rsem, device_id=dev, device_id_type=MESH)
 
     barrier = pltpu.get_barrier_semaphore()
-    peers = [zpeer(o) for o in (1, 2, 3, 13, 14, 15)] + [xpeer(d) for d in (1, 2, 3)] + [ypeer(d) for d in (1, 2, 3)] + [sibling]
+    peers = [zpeer(o) for o in GREETED] + [xpeer(d) for d in (1, 2, 3)] + [ypeer(d) for d in (1, 2, 3)] + [sibling]
     for dev in peers:
         pl.semaphore_signal(barrier, inc=1, device_id=dev, device_id_type=MESH)
 
-    phon_copy = pltpu.make_async_copy(phon_in.at[0], phon.at[0], in_sem.at[0])
+    phon_copy = pltpu.make_async_copy(phon_in.at[0], phon.at[0, :, pl.ds(0, 1024)], in_sem.at[0])
     dur_load = pltpu.make_async_copy(dur_in, dur_row, in_sem.at[1])
     w2_copy = pltpu.make_async_copy(out_w, w2_own, in_sem.at[2])
     gain_copy = pltpu.make_async_copy(gain_in, gain, in_sem.at[3])
@@ -54,9 +55,11 @@
     for d in (phon_copy, dur_load, w2_copy, gain_copy, w_copy):
         d.start()
 
-    dur_all[0] = jnp.zeros((1, 128), jnp.int32)
+    dur_wide[...] = jnp.zeros_like(dur_wide)
     dur_load.wait()
-    dur_all[0, :, 0:16] = dur_row[...]
+    dur_wide[:, 0:16] = dur_row[...]
+    top = lax.broadcasted_iota(jnp.int32, (16, 128), 0) == 0
+    phon[0, :, 1024:1152] = jnp.where(top, dur_wide[...].astype(F32), 0.0).astype(BF)
     w2_copy.wait()
     w2[y, x, c, 0, :, 0:128] = w2_own[0:16]
     w2[y, x, c, 1, :, 0:128] = w2_own[16:32]
@@ -65,7 +68,7 @@
     def phon_part(o, part):
         if part is None:
             return phon.at[ORDER.index(o)]
-        return phon.at[ORDER.index(o), :, pl.ds(512 * part, 512)]
+        return phon.at[ORDER.index(o), :, pl.ds(640 * part, 640 - 128 * part)]
 
     def w2_part(o, part):
         lanes = pl.ds(128 * ORDER.index(o), 128)
@@ -73,28 +76,24 @@
             return w2.at[y, x, c, :, :, lanes]
         return w2.at[y, x, c, part, :, lanes]
 
-    def dur_part(o, part):
-        return dur_all.at[o]
-
-    def gather(place, ssem, rsem, halves=True):
+    def gather(place, ssem, rsem):
         def copy(held, to, there):
-            part = None if there != 8 or not halves else (0 if held == 6 else 1)
+            part = None if there != 8 else (0 if held < 8 else 1)
             i = 0 if part == 1 else there
             return remote(place(held, part), place(there, part), ssem.at[i], rsem.at[i], zpeer(to))
 
         direct = {o: [copy(0, o, o)] for o in DIRECT}
-        onward = {held: [copy(held, to, there) for to, there in jobs if halves or (held, there) != (10, 8)]
-                  for held, jobs in ONWARD.items()}
+        onward = {held: [copy(held, to, there) for to, there in jobs] for held, jobs in ONWARD.items()}
         arrival = dict(direct)
         for held, jobs in ONWARD.items():
-            for job, d in zip(jobs[::-1], onward[held][::-1]):
+            for job, d in zip(jobs, onward[held]):
                 arrival[job[1]] = arrival.get(job[1], []) + [d]
         return direct, onward, arrival
 
     pl.semaphore_wait(barrier, len(peers))
 
-    gathers = [gather(w2_part, ws, wr), gather(phon_part, ps, pr), gather(dur_part, ds, dr, False)]
-    cols, rows, durs = [g[2] for g in gathers]
+    gathers = [gather(phon_part, ps, pr), gather(w2_part, ws, wr)]
+    rows, cols = [g[2] for g in gathers]
 
     def arrive(chunks, which):
         for o in which:
@@ -104,14 +103,15 @@
     for direct, _, _ in gathers:
         for o in DIRECT:
             direct[o][0].start()
-    for held in ONWARD:
+    for helds in (DIRECT[0:2], (6, 10)):
         for _, onward, arrival in gathers:
-            arrive(arrival, (held,))
-            for d in onward[held]:
-                d.start()
+            for held in helds:
+                arrive(arrival, (held,))
+                for d in onward[held]:
+                    d.start()
 
     def products(begin, end):
-        rows = phon[begin:end].reshape(16 * (end - begin), 1024)
+        rows = phon[begin:end, :, 0:1024].reshape(16 * (end - begin), 1024)
         for k in range(0, TAPS, 2):
             taps = [w[t] for t in range(k, min(k + 2, TAPS))]
             cols = jnp.concatenate(taps, axis=1) if len(taps) > 1 else taps[0]
@@ -159,15 +159,21 @@
             d.wait_recv()
             onward.start()
 
-    spread_first(0)
     w_copy.wait()
     for begin, end in GROUPS[0:2]:
         arrive(rows, ORDER[begin:end])
         products(begin, end)
-    spread_first(1)
-
-    arrive(durs, range(NZ))
-    lengths = jnp.concatenate([dur_all[o] for o in range(NZ)], axis=0).astype(F32).astype(BF)
+    spread_first(0)
+
+    begin, end = GROUPS[2]
+    arrive(rows, ORDER[begin:end])
+    chunk = lax.broadcasted_iota(jnp.int32, (NZ, 256), 0)
+    line = lax.broadcasted_iota(jnp.int32, (NZ, 256), 1)
+    pick_line = jnp.zeros((NZ, 256), F32)
+    for i, o in enumerate(ORDER):
+        pick_line = jnp.where((chunk == o) & (line == 16 * i), 1.0, pick_line)
+    lengths = jnp.dot(pick_line.astype(BF), phon[:, :, 1024:1152].reshape(256, 128),
+                      preferred_element_type=F32).astype(BF)
     col = lax.broadcasted_iota(jnp.int32, (1, 256), 1)
     slot, place = col // 16, lax.rem(col, 16)
     col_off = jnp.zeros_like(col)
@@ -191,8 +197,6 @@
         frame = (lax.broadcasted_iota(jnp.int32, (count, 256), 0) + first).astype(F32)
         return jnp.where((frame >= starts) & (frame < ends), 1.0, 0.0).astype(BF)
 
-    begin, end = GROUPS[2]
-    arrive(rows, ORDER[begin:end])
     products(begin, end)
 
     def hidden(o):
@@ -217,15 +221,15 @@
         hid_copy(o).start()
         return carry
 
-    lax.fori_loop(0, 3, send_hidden, 0)
+    lax.fori_loop(0, 4, send_hidden, 0)
+    spread_first(1)
+    lax.fori_loop(4, 8, send_hidden, 0)
+    lax.fori_loop(9, NZ, send_hidden, 0)
     spread_second(0)
-    lax.fori_loop(3, 6, send_hidden, 0)
     spread_second(1)
-    lax.fori_loop(6, 8, send_hidden, 0)
-    lax.fori_loop(9, NZ, send_hidden, 0)
     hid_in[0] = hidden(0)
 
-    acc[...] = jnp.dot(one_hot(z * 128, 128), phon[...].reshape(256, 1024), preferred_element_type=F32)
+    acc[...] = jnp.dot(one_hot(z * 128, 128), phon[:, :, 0:1024].reshape(256, 1024), preferred_element_type=F32)
 
     for i in range(len(WAVES)):
         spread_cross(i)
@@ -234,7 +238,7 @@
             d.wait_recv()
 
     order = [(8 + 7 * i) % NZ for i in range(NZ)]
-    groups = (order[0:4], order[4:8], [0] + order[9:12], order[12:16])
+    groups = (order[0:4], order[4:8], [0] + order[9:12], order[12:14], order[14:16])
     for group in groups:
         for o in group:
             if o:
@@ -255,7 +259,7 @@
         out[0, rows, :] = (centered * lax.rsqrt(spread + 1e-5) * gain[...]).astype(BF)
         return carry
 
-    lax.fori_loop(0, 8, norm, 0)
+    lax.fori_loop(0, 8, norm, 0, unroll=True)
 
     for direct, onward, _ in gathers:
         for jobs in [*direct.values(), *onward.values()]:
@@ -277,9 +281,9 @@
         in_specs=[pl.BlockSpec(memory_space=pltpu.HBM)] * 5,
         out_specs=vmem,
         scratch_shapes=[
-            pltpu.VMEM((NZ, 16, 1024), BF),
+            pltpu.VMEM((NZ, 16, 1152), BF),
             pltpu.VMEM((1, 16), jnp.int32),
-            pltpu.VMEM((NZ, 1, 128), jnp.int32),
+            pltpu.VMEM((1, 128), jnp.int32),
             pltpu.VMEM((TAPS, 1024, 128), BF),
             pltpu.VMEM((32, 128), BF),
             pltpu.VMEM((1, 1024), F32),
@@ -288,7 +292,7 @@
             pltpu.VMEM((NZ, 128, 128), BF),
             pltpu.VMEM((NZ, 128, 128), BF),
             pltpu.VMEM((128, 1024), F32),
-            sems((5,)), sems((16,)), sems((16,)), sems((16,)), sems((16,)), sems((16,)), sems((16,)),
+            sems((5,)), sems((16,)), sems((16,)), sems((16,)), sems((16,)),
             sems((2, 13)), sems((2, 13)), sems((2, 8)), sems((2, 8)), sems((16,)), sems((16,)),
         ],
         compiler_params=pltpu.CompilerParams(

time: 57.8 us -> 55.1 us (0.953)
  the two profiles are of different devices: /device:TPU:6 before, /device:TPU:1 now
where the time goes in v5:
time: 55.1 us; the launch traced here: 54.9 us
  Pallas kernels  54.2 us (98%)
  local copies, waits for them, and re-layouts  0.71 us (1%)
    pallas_call x1, Pallas kernels, on_device(): pl.pallas_call(kernel, out_shape=pltpu.VMEM((1, 128, 1024), BF), in_specs...  54.2 us

profile of v5, /device:TPU:1, one launch (start us, length us, event | category | flops | bytes accessed | tf_op | source)
XLA Modules:
  0.0 54.9 jit_solution(12210905778142144289)
XLA Ops:
  0.0 54.2 %shard_map.55 = bf16[1,128,1024]{2,1,0:T(8,128)(2,1)S(1)} custom-call(bf16[1,16,1024]{2,1,0:T(8,128)(2,1)} %phon_in.1, s32[1,16]{1,0:T(1,128)} %dur_in.1, bf16[9,1024,128]{2,1,0:T(8,128)(2,1)} %conv_w.1, bf16[32,128]{1,0:T(8,128)(2,1)} %bitcast.2, f32[1,1024]{1,0:T(1,128)} %bitcast.3), custom_call_target="tpu_custom_call" | custom-call | flops 4000000000 | bytes 4000000 | tf_op jit(solution)/shard_map/pallas_call | solution.py:278
  54.2 0.7 %copy.7 = bf16[1,128,1024]{2,1,0:T(8,128)(2,1)} copy(bf16[1,128,1024]{2,1,0:T(8,128)(2,1)S(1)} %shard_map.55) | data formatting | bytes 524288

commit v6 on v4

--- a/solution.py
+++ b/solution.py
@@ -12,6 +12,7 @@
 DIRECT = (3, 13, 1, 15)
 ONWARD = {3: ((3, 6), (1, 4), (15, 2)), 13: ((13, 10), (15, 12), (1, 14)),
           6: ((2, 8), (1, 7), (15, 5)), 10: ((14, 8), (15, 9), (1, 11))}
+GREETED = (1, 2, 3, 13, 14, 15)
 GROUPS = ((0, 5), (5, 11), (11, 16))
 WAVES = ((0, 11), (11, 16))
 TAPS = 9
@@ -42,8 +43,9 @@
             src_ref=src, dst_ref=dst, send_sem=ssem, recv_sem=rsem, device_id=dev, device_id_type=MESH)
 
     barrier = pltpu.get_barrier_semaphore()
-    peers = [zpeer(o) for o in (1, 2, 3, 13, 14, 15)] + [xpeer(d) for d in (1, 2, 3)] + [ypeer(d) for d in (1, 2, 3)] + [sibling]
-    for dev in peers:
+    around = [zpeer(o) for o in GREETED]
+    across = [xpeer(d) for d in (1, 2, 3)] + [ypeer(d) for d in (1, 2, 3)] + [sibling]
+    for dev in around:
         pl.semaphore_signal(barrier, inc=1, device_id=dev, device_id_type=MESH)
 
     phon_copy = pltpu.make_async_copy(phon_in.at[0], phon.at[0], in_sem.at[0])
@@ -51,15 +53,14 @@
     w2_copy = pltpu.make_async_copy(out_w, w2_own, in_sem.at[2])
     gain_copy = pltpu.make_async_copy(gain_in, gain, in_sem.at[3])
     w_copy = pltpu.make_async_copy(conv_w, w, in_sem.at[4])
-    for d in (phon_copy, dur_load, w2_copy, gain_copy, w_copy):
+    for d in (dur_load, phon_copy, w2_copy, w_copy, gain_copy):
         d.start()
+    for dev in across:
+        pl.semaphore_signal(barrier, inc=1, device_id=dev, device_id_type=MESH)
 
     dur_all[0] = jnp.zeros((1, 128), jnp.int32)
     dur_load.wait()
     dur_all[0, :, 0:16] = dur_row[...]
-    w2_copy.wait()
-    w2[y, x, c, 0, :, 0:128] = w2_own[0:16]
-    w2[y, x, c, 1, :, 0:128] = w2_own[16:32]
     phon_copy.wait()
 
     def phon_part(o, part):
@@ -78,12 +79,12 @@
 
     def gather(place, ssem, rsem, halves=True):
         def copy(held, to, there):
-            part = None if there != 8 or not halves else (0 if held == 6 else 1)
+            part = None if there != 8 or not halves else (0 if held < 8 else 1)
             i = 0 if part == 1 else there
             return remote(place(held, part), place(there, part), ssem.at[i], rsem.at[i], zpeer(to))
 
         direct = {o: [copy(0, o, o)] for o in DIRECT}
-        onward = {held: [copy(held, to, there) for to, there in jobs if halves or (held, there) != (10, 8)]
+        onward = {held: [copy(held, to, there) for to, there in (jobs if halves or held != 10 else jobs[1:])]
                   for held, jobs in ONWARD.items()}
         arrival = dict(direct)
         for held, jobs in ONWARD.items():
@@ -91,24 +92,30 @@
                 arrival[job[1]] = arrival.get(job[1], []) + [d]
         return direct, onward, arrival
 
-    pl.semaphore_wait(barrier, len(peers))
-
-    gathers = [gather(w2_part, ws, wr), gather(phon_part, ps, pr), gather(dur_part, ds, dr, False)]
-    cols, rows, durs = [g[2] for g in gathers]
+    pl.semaphore_wait(barrier, len(around) + len(across))
+
+    gathers = [gather(phon_part, ps, pr), gather(dur_part, ds, dr, False), gather(w2_part, ws, wr)]
+    rows, durs, cols = [g[2] for g in gathers]
 
     def arrive(chunks, which):
         for o in which:
             for d in chunks.pop(o, []):
                 d.wait_recv()
 
-    for direct, _, _ in gathers:
+    for direct, _, _ in gathers[0:2]:
         for o in DIRECT:
             direct[o][0].start()
-    for held in ONWARD:
+    w2_copy.wait()
+    w2[y, x, c, 0, :, 0:128] = w2_own[0:16]
+    w2[y, x, c, 1, :, 0:128] = w2_own[16:32]
+    for o in DIRECT:
+        gathers[2][0][o][0].start()
+    for helds in (DIRECT[0:2], (6, 10)):
         for _, onward, arrival in gathers:
-            arrive(arrival, (held,))
-            for d in onward[held]:
-                d.start()
+            for held in helds:
+                arrive(arrival, (held,))
+                for d in onward[held]:
+                    d.start()
 
     def products(begin, end):
         rows = phon[begin:end].reshape(16 * (end - begin), 1024)
@@ -159,15 +166,15 @@
             d.wait_recv()
             onward.start()
 
-    spread_first(0)
     w_copy.wait()
     for begin, end in GROUPS[0:2]:
         arrive(rows, ORDER[begin:end])
         products(begin, end)
-    spread_first(1)
+    spread_first(0)
 
     arrive(durs, range(NZ))
     lengths = jnp.concatenate([dur_all[o] for o in range(NZ)], axis=0).astype(F32).astype(BF)
+    begin, end = GROUPS[2]
     col = lax.broadcasted_iota(jnp.int32, (1, 256), 1)
     slot, place = col // 16, lax.rem(col, 16)
     col_off = jnp.zeros_like(col)
@@ -191,7 +198,6 @@
         frame = (lax.broadcasted_iota(jnp.int32, (count, 256), 0) + first).astype(F32)
         return jnp.where((frame >= starts) & (frame < ends), 1.0, 0.0).astype(BF)
 
-    begin, end = GROUPS[2]
     arrive(rows, ORDER[begin:end])
     products(begin, end)
 
@@ -217,12 +223,12 @@
         hid_copy(o).start()
         return carry
 
-    lax.fori_loop(0, 3, send_hidden, 0)
+    lax.fori_loop(0, 4, send_hidden, 0)
+    spread_first(1)
+    lax.fori_loop(4, 8, send_hidden, 0)
+    lax.fori_loop(9, NZ, send_hidden, 0)
     spread_second(0)
-    lax.fori_loop(3, 6, send_hidden, 0)
     spread_second(1)
-    lax.fori_loop(6, 8, send_hidden, 0)
-    lax.fori_loop(9, NZ, send_hidden, 0)
     hid_in[0] = hidden(0)
 
     acc[...] = jnp.dot(one_hot(z * 128, 128), phon[...].reshape(256, 1024), preferred_element_type=F32)
@@ -234,7 +240,7 @@
             d.wait_recv()
 
     order = [(8 + 7 * i) % NZ for i in range(NZ)]
-    groups = (order[0:4], order[4:8], [0] + order[9:12], order[12:16])
+    groups = (order[0:4], order[4:8], [0] + order[9:12], order[12:14], order[14:16])
     for group in groups:
         for o in group:
             if o:
@@ -255,7 +261,7 @@
         out[0, rows, :] = (centered * lax.rsqrt(spread + 1e-5) * gain[...]).astype(BF)
         return carry
 
-    lax.fori_loop(0, 8, norm, 0)
+    lax.fori_loop(0, 8, norm, 0, unroll=True)
 
     for direct, onward, _ in gathers:
         for jobs in [*direct.values(), *onward.values()]:

time: 57.8 us -> 54.8 us (0.948)
  the two profiles are of different devices: /device:TPU:6 before, /device:TPU:1 now
where the time goes in v6:
time: 54.8 us; the launch traced here: 54.7 us
  Pallas kernels  54 us (99%)
  local copies, waits for them, and re-layouts  0.71 us (1%)
    pallas_call x1, Pallas kernels, on_device(): pl.pallas_call(kernel, out_shape=pltpu.VMEM((1, 128, 1024), BF), in_specs...  54 us

profile of v6, /device:TPU:1, one launch (start us, length us, event | category | flops | bytes accessed | tf_op | source)
XLA Modules:
  0.0 54.7 jit_solution(12403932818683559803)
XLA Ops:
  0.0 54.0 %shard_map.55 = bf16[1,128,1024]{2,1,0:T(8,128)(2,1)S(1)} custom-call(bf16[1,16,1024]{2,1,0:T(8,128)(2,1)} %phon_in.1, s32[1,16]{1,0:T(1,128)} %dur_in.1, bf16[9,1024,128]{2,1,0:T(8,128)(2,1)} %conv_w.1, bf16[32,128]{1,0:T(8,128)(2,1)} %bitcast.2, f32[1,1024]{1,0:T(1,128)} %bitcast.3), custom_call_target="tpu_custom_call" | custom-call | flops 4000000000 | bytes 4000000 | tf_op jit(solution)/shard_map/pallas_call | solution.py:280
  54.0 0.7 %copy.7 = bf16[1,128,1024]{2,1,0:T(8,128)(2,1)} copy(bf16[1,128,1024]{2,1,0:T(8,128)(2,1)S(1)} %shard_map.55) | data formatting | bytes 524288

commit v7 on v6

--- a/solution.py
+++ b/solution.py
@@ -214,13 +214,15 @@
                 total = total + got[k + 1:k + 129, 128:256]
         return jnp.maximum(total, 0.0).astype(BF)
 
-    def hid_copy(o):
-        return remote(hid_out.at[o], hid_in.at[o], hs.at[o], hr.at[o], zpeer(o))
+    def hid_copies(o):
+        return [remote(hid_out.at[o, pl.ds(64 * k, 64)], hid_in.at[o, pl.ds(64 * k, 64)], hs.at[k, o], hr.at[k, o], zpeer(o))
+                for k in (0, 1)]
 
     def send_hidden(i, carry):
         o = lax.rem(8 + 7 * i, NZ)
         hid_out[o] = hidden(o)
-        hid_copy(o).start()
+        for d in hid_copies(o):
+            d.start()
         return carry
 
     lax.fori_loop(0, 4, send_hidden, 0)
@@ -244,7 +246,8 @@
     for group in groups:
         for o in group:
             if o:
-                hid_copy(o).wait_recv()
+                for d in hid_copies(o):
+                    d.wait_recv()
         left = jnp.concatenate([hid_in[o] for o in group], axis=1)
         slots = [ORDER.index(o) for o in group]
         right = jnp.concatenate(
@@ -271,7 +274,8 @@
         for d in first + second + cross:
             d.wait_send()
     for o in range(1, NZ):
-        hid_copy(o).wait_send()
+        for d in hid_copies(o):
+            d.wait_send()
 
 
 def on_device(phonemes, durations, conv_weight, out_weight, norm_gain):
@@ -295,7 +299,7 @@
             pltpu.VMEM((NZ, 128, 128), BF),
             pltpu.VMEM((128, 1024), F32),
             sems((5,)), sems((16,)), sems((16,)), sems((16,)), sems((16,)), sems((16,)), sems((16,)),
-            sems((2, 13)), sems((2, 13)), sems((2, 8)), sems((2, 8)), sems((16,)), sems((16,)),
+            sems((2, 13)), sems((2, 13)), sems((2, 8)), sems((2, 8)), sems((2, 16)), sems((2, 16)),
         ],
         compiler_params=pltpu.CompilerParams(
             collective_id=0, has_side_effects=True, vmem_limit_bytes=63 * 1024 * 1024),

time: 54.8 us -> 55.1 us (level)
  no operation moved by 1% of the time
where the time goes in v7:
time: 55.1 us; the launch traced here: 55 us
  Pallas kernels  54.3 us (99%)
  local copies, waits for them, and re-layouts  0.71 us (1%)
    pallas_call x1, Pallas kernels, on_device(): pl.pallas_call(kernel, out_shape=pltpu.VMEM((1, 128, 1024), BF), in_specs...  54.3 us

profile of v7, /device:TPU:1, one launch (start us, length us, event | category | flops | bytes accessed | tf_op | source)
XLA Modules:
  0.0 55.0 jit_solution(13987046624450872881)
XLA Ops:
  0.0 54.3 %shard_map.55 = bf16[1,128,1024]{2,1,0:T(8,128)(2,1)S(1)} custom-call(bf16[1,16,1024]{2,1,0:T(8,128)(2,1)} %phon_in.1, s32[1,16]{1,0:T(1,128)} %dur_in.1, bf16[9,1024,128]{2,1,0:T(8,128)(2,1)} %conv_w.1, bf16[32,128]{1,0:T(8,128)(2,1)} %bitcast.2, f32[1,1024]{1,0:T(1,128)} %bitcast.3), custom_call_target="tpu_custom_call" | custom-call | flops 4000000000 | bytes 4000000 | tf_op jit(solution)/shard_map/pallas_call | solution.py:284
  54.3 0.7 %copy.7 = bf16[1,128,1024]{2,1,0:T(8,128)(2,1)} copy(bf16[1,128,1024]{2,1,0:T(8,128)(2,1)S(1)} %shard_map.55) | data formatting | bytes 524288
